TPU v7x, 32 devices: a whole 2x2x4 slice. The times are simulated.
32 devices in a mesh: grp: 2 (over x), seq: 4 (over y, core), pair: 4 (over z).
Axes of the slice: x: 2, y: 2, z: 4, core: 2. Of those that a mesh axis runs over, the one named last changes fastest.
Arguments:
- seq_input: bfloat16 [8, 256, 1536], P(('grp', 'pair'), 'seq'), parts along dimension 0, may hold values from -6 to 6
- skip_input: bfloat16 [8, 512, 1536], P(('grp', 'pair'), 'seq'), parts along dimension 0, may hold values from -6 to 6
- norm_gain: float32 [1536], replicated, may hold values from 0.5 to 1.5
- query_weight: bfloat16 [1536, 512], replicated, may hold values from -2 to 2
- key_weight: bfloat16 [1536, 512], replicated, may hold values from -2 to 2
- value_weight: bfloat16 [1536, 1536], replicated, may hold values from -0.15625 to 0.15625
- conv_weight: float32 [3, 1536], replicated, may hold values from -3 to 3
- head_weight: bfloat16 [1536, 4096], P(None, 'pair'), may hold values from -0.15625 to 0.15625
- head_bias: float32 [4096], P('pair'), may hold values from -4 to 4
- exon_start: int32 [4, 64], P('grp'), parts along dimension 0, may hold values from 0 to 496
- exon_length: int32 [4, 64], P('grp'), parts along dimension 0, may hold values from 1 to 16
- exon_gene: int32 [4, 64], P('grp'), parts along dimension 0, may hold values from 0 to 7, as said below
- gene_order: int32 [4, 8], P('grp'), parts along dimension 0, may hold values from 0 to 7, each once within a row
Outputs:
- scores: float32 [4, 8, 4096], P('grp', 'seq', 'pair'), parts along dimension 0
There are 2 independent parts, one for each index of `grp`. A program takes and returns all parts, laid end to end along the dimension named above; an argument that names none is the same for every part. Nothing has to cross between parts.
Inputs may be any that keep to these rules, and one draw needn't show every extreme that they name: `exon_gene`: every gene has at least one exon record. `gene_order`: each row names every gene once; the device at index s along seq owns positions s * 2 to (s + 1) * 2 - 1.
All inputs are finite; a program needn't handle non-finite values.
Results may differ from a plain program's by a relative error of at most 0.012.
Values may be sent and summed in bfloat16 or wider, within the bound.
A program may use at most 128 MiB of HBM per device.

v0:
```python
import math

import jax
import jax.numpy as jnp
from jax import lax
from jax.sharding import PartitionSpec as P

HEADS = 8
KEY = 64
VALUE = 192


EPSILON = 1e-05


def with_halo(block, sides, width):
    for axis, dim in sides:
        count = lax.axis_size(axis)
        forward = [(i, i + 1) for i in range(count - 1)]
        backward = [(target, source) for source, target in forward]
        low = lax.ppermute(
            lax.slice_in_dim(block, block.shape[dim] - width, None, axis=dim), axis, forward
        )
        high = lax.ppermute(lax.slice_in_dim(block, 0, width, axis=dim), axis, backward)
        block = jnp.concatenate([low, block, high], axis=dim)
    return block


def layer_normed(rows, norm_gain):
    rows_wide = rows.astype(jnp.float32)
    center = jnp.mean(rows_wide, axis=-1, keepdims=True)
    spread_sq = jnp.mean(jnp.square(rows_wide - center), axis=-1, keepdims=True)
    return ((rows_wide - center) * lax.rsqrt(spread_sq + EPSILON) * norm_gain).astype(jnp.bfloat16)


def gene_masks(exon_start, exon_length, exon_gene, gene_order, positions):
    lower = exon_start[:, :, None]
    upper = lower + exon_length[:, :, None]
    inside = ((positions[None, None, :] >= lower) & (positions[None, None, :] < upper)).astype(
        jnp.float32
    )
    chosen = (exon_gene[:, None, :] == gene_order[:, :, None]).astype(jnp.float32)
    return jnp.einsum("vpe,veb->vpb", chosen, inside, precision=lax.Precision.HIGHEST)


def absorb_keys(running, query_rows, key_rows, value_rows, head_count, inv_root):
    row_peak, denom, accum = running
    row_total = key_rows.shape[0]
    for lower in range(0, row_total, 512):
        upper = min(lower + 512, row_total)
        key_block = key_rows[lower:upper].reshape(upper - lower, head_count, KEY)
        value_block = value_rows[lower:upper].reshape(upper - lower, head_count, VALUE)
        logits = (
            jnp.einsum("qhk,phk->hqp", query_rows, key_block, preferred_element_type=jnp.float32)
            * inv_root
        )
        new_peak = jnp.maximum(row_peak, jnp.max(logits, axis=-1))
        rescale = jnp.exp(row_peak - new_peak)
        expo = jnp.exp(logits - new_peak[:, :, None])
        denom = denom * rescale + jnp.sum(expo, axis=-1)
        partial_out = jnp.einsum(
            "hqp,phv->qhv",
            expo.astype(jnp.bfloat16),
            value_block,
            preferred_element_type=jnp.float32,
        )
        accum = accum * jnp.transpose(rescale)[:, :, None] + partial_out
        row_peak = new_peak
    return (row_peak, denom, accum)


def empty_state(head_count, query_count):
    return (
        jnp.full((head_count, query_count), -1e30, jnp.float32),
        jnp.zeros((head_count, query_count), jnp.float32),
        jnp.zeros((query_count, head_count, VALUE), jnp.float32),
    )


def body(
    seq_input,
    skip_input,
    norm_gain,
    query_weight,
    key_weight,
    value_weight,
    conv_weight,
    head_weight,
    head_bias,
    exon_start,
    exon_length,
    exon_gene,
    gene_order,
):
    rows = seq_input[0]
    bin_count = rows.shape[0]
    width = rows.shape[1]
    inv_root = 1.0 / math.sqrt(KEY)
    normed = layer_normed(rows, norm_gain)
    queries = jnp.dot(normed, query_weight, preferred_element_type=jnp.float32).astype(jnp.bfloat16)
    keys_local = jnp.dot(normed, key_weight, preferred_element_type=jnp.float32).astype(
        jnp.bfloat16
    )
    values_local = jnp.dot(normed, value_weight, preferred_element_type=jnp.float32).astype(
        jnp.bfloat16
    )
    query_rows = queries.reshape(bin_count, HEADS, KEY)
    row_peak, denom, accum = absorb_keys(
        empty_state(HEADS, bin_count),
        query_rows,
        lax.all_gather(keys_local[None], "seq", axis=1, tiled=True)[0],
        lax.all_gather(values_local[None], "seq", axis=1, tiled=True)[0],
        HEADS,
        inv_root,
    )
    attention = (accum / jnp.transpose(denom)[:, :, None]).reshape(bin_count, width)
    attended = (rows.astype(jnp.float32) + attention).astype(jnp.bfloat16)
    upsampled = jnp.repeat(attended.astype(jnp.float32), 2, axis=0) + skip_input[0].astype(
        jnp.float32
    )
    padded = with_halo(upsampled, (("seq", 0),), 1)
    convolved = (
        conv_weight[0] * padded[:-2] + conv_weight[1] * padded[1:-1] + conv_weight[2] * padded[2:]
    )
    feature = jax.nn.gelu(convolved, approximate=True).astype(jnp.bfloat16)
    out_rows = feature.shape[0]
    positions = lax.axis_index("seq") * out_rows + jnp.arange(out_rows, dtype=jnp.int32)
    seq_masks = jnp.repeat(
        gene_masks(exon_start, exon_length, exon_gene, gene_order, positions), 2, axis=0
    )
    full_weight, full_bias = (
        lax.all_gather(head_weight, "pair", axis=1, tiled=True),
        lax.all_gather(head_bias.astype(jnp.bfloat16), "pair", axis=0, tiled=True).astype(
            head_bias.dtype
        ),
    )
    predicted = jax.nn.softplus(
        jnp.dot(feature, full_weight, preferred_element_type=jnp.float32) + full_bias
    )
    own_mask = lax.dynamic_index_in_dim(seq_masks, lax.axis_index("pair"), 0, keepdims=False)
    own_cover = jnp.dot(own_mask, predicted, precision=lax.Precision.HIGHEST)[None]
    gene_cover = lax.psum_scatter(own_cover, "seq", scatter_dimension=1, tiled=True)
    coverage = lax.all_to_all(gene_cover, "pair", split_axis=2, concat_axis=0, tiled=True)
    return jnp.log1p(coverage[1::2]) - jnp.log1p(coverage[0::2])


def solution(mesh):
    placed = (
        P(("grp", "pair"), "seq", None),
        P(("grp", "pair"), "seq", None),
        P(),
        P(),
        P(),
        P(),
        P(),
        P(None, "pair"),
        P("pair"),
        P("grp", None),
        P("grp", None),
        P("grp", None),
        P("grp", None),
    )
    return jax.shard_map(
        body, mesh=mesh, in_specs=placed, out_specs=P("grp", "seq", "pair"), check_vma=False
    )
```

profile of v0, /device:TPU:0, one launch (start us, length us, event | category | flops | bytes accessed | tf_op | source)
XLA Modules:
  0.0 322.8 jit_solution(7170680380619183803)
XLA Ops:
  6.5 0.0 copy-start
  6.5 0.0 all-gather.4.cloned.1.call-start
  6.5 0.7 all-gather.4.cloned.1.call-update
  7.3 0.0 copy-start.2
  7.3 0.0 all-reduce.3.cloned.1.call-start
  7.3 0.3 copy-done.1
  7.6 0.1 convert_reduce_fusion
  7.7 0.2 fusion.28
  8.0 0.1 copy-done
  8.0 0.0 copy-done.5
  8.0 0.4 convolution_convert_fusion.1
  8.5 7.7 %all-gather = bf16[256,512]{1,0:T(8,128)(2,1)} all-gather(bf16[64,512]{1,0:T(8,128)(2,1)S(1)} %convolution_convert_fusion.1), channel_id=2, replica_groups=mesh['grp'=2,'seq'=4,'pair'=4] {'seq'}, dimensions={0}, use_global_device_ids=true | all-gather | bytes 327680 | tf_op jit(solution)/shard_map/all_gather | solution.py:111
  16.1 1.8 copy.23
  17.9 0.0 copy-done.2
  17.9 0.4 convolution_convert_fusion.2
  18.4 0.1 reshape.44
  18.5 4.1 %convolution_convert_fusion = bf16[64,1536]{1,0:T(8,128)(2,1)S(1)} fusion(bf16[1536,1536]{1,0:T(8,128)(2,1)} %param.18, bf16[1,64,1536]{2,1,0:T(8,128)(2,1)S(1)} %copy-done.1, f32[1536]{0:T(1024)S(1)} %copy-done.5, f32[64]{0:T(128)S(1)} %add_rsqrt_fusion, f32[64]{0:T(128)S(1)} %broadcast_multiply_fusion), kind=kOutput, calls=%fused_computation.3 | convolution fusion | flops 302579712 | bytes 5118464 | tf_op jit(solution)/shard_map/dot_general | solution.py:104
  22.6 0.0 copy-start.3
  22.6 8.8 %all-gather.1 = bf16[256,1536]{1,0:T(8,128)(2,1)S(1)} all-gather(bf16[64,1536]{1,0:T(8,128)(2,1)S(1)} %convolution_convert_fusion), channel_id=3, replica_groups=mesh['grp'=2,'seq'=4,'pair'=4] {'seq'}, dimensions={0}, use_global_device_ids=true | all-gather | bytes 983040 | tf_op jit(solution)/shard_map/all_gather | solution.py:112
  31.4 1.2 copy.25
  32.6 0.0 copy-done.3
  32.6 0.3 fusion.63
  32.9 0.3 fusion.25
  33.2 1.5 fusion.7
  34.8 0.3 copy.26
  35.1 0.2 reshape.45
  35.3 0.0 copy-start.4
  35.3 0.0 copy-start.7
  35.3 0.0 copy-start.8
  35.4 0.0 copy-start.9
  35.4 0.3 broadcast_in_dim.19
  35.6 0.0 copy-start.6
  35.7 0.5 reshape.46
  36.2 0.1 copy-done.4
  36.3 0.1 convert_add_fusion
  36.4 2.3 collective-permute-start
  38.6 1.3 collective-permute-start.1
  39.9 0.0 copy-done.7
  40.0 0.0 copy-done.8
  40.0 0.0 copy-done.9
  40.0 0.9 fusion.43
  40.9 0.9 slice_reduce_fusion.2
  41.8 0.0 copy-done.6
  41.8 19.1 %all_gather.15 = bf16[4096]{0:T(1024)(128)(2,1)S(1)} all-gather(bf16[1024]{0:T(1024)(128)(2,1)S(1)} %convert_element_type.57), channel_id=1, replica_groups=mesh['grp'=2,'seq'=4,'pair'=4] {'pair'}, dimensions={0}, use_global_device_ids=true | all-gather | bytes 10240 | tf_op jit(solution)/shard_map/all_gather | solution.py:133
  60.9 0.0 collective-permute-done
  60.9 0.0 collective-permute-done.1
  60.9 169.1 %all-gather.4.cloned.1.call-done = bf16[1536,4096]{1,0:T(8,128)(2,1)} async-done(((bf16[1536,1024]{1,0:T(8,128)(2,1)}), bf16[1536,4096]{1,0:T(8,128)(2,1)}) %all-gather.4.cloned.1.call-update) | async-done | bytes 12582928 | tf_op jit(solution)/shard_map/all_gather | solution.py:132
  230.0 6.7 %convolution_add_fusion = f32[128,4096]{1,0:T(8,128)S(1)} fusion(bf16[1536,4096]{1,0:T(8,128)(2,1)} %all-gather.4.cloned.1.call-done, f32[4096]{0:T(1024)S(1)} %convert_element_type.58, f32[1,1536]{1,0:T(1,128)S(1)} %collective-permute-done.1, f32[128,1536]{1,0:T(8,128)S(1)} %convert_add_fusion, f32[1,1536]{1,0:T(1,128)S(1)} %collective-permute-done, ...), kind=kOutput, calls=%fused_computation.1 | convolution fusion | flops 1614282752 | bytes 15513600 | tf_op jit(solution)/shard_map/dot_general | solution.py:138
  236.8 0.0 copy-start.10
  236.8 2.8 convolution_bitcast_fusion
  239.6 0.0 all-reduce.3.cloned.1.call-update
  239.6 0.0 copy-done.10
  239.6 0.6 dynamic-slice
  240.9 28.5 %all-reduce.3.cloned.1.call-done = f32[1,8,4096]{2,1,0:T(8,128)} async-done(((f32[1,8,4096]{2,1,0:T(8,128)}), f32[1,8,4096]{2,1,0:T(8,128)}) %all-reduce.3.cloned.1.call-update) | async-done | bytes 131088
  269.4 0.9 constant_dynamic-slice_fusion
  270.3 3.6 %copy.27 = f32[1,2,4096]{1,0,2:T(1,128)} copy(f32[1,2,4096]{2,1,0:T(2,128)S(1)} %constant_dynamic-slice_fusion) | data formatting | bytes 65536 | tf_op jit(solution)/shard_map/reduce_scatter | solution.py:142
  273.9 0.5 broadcast.52
  274.4 20.4 %reduce.7 = f32[4096,2]{1,0:T(8,128)} reduce(f32[4096,1,2]{2,1,0:T(1,128)} %bitcast.61, f32[]{:T(128)} %broadcast.52), dimensions={1}, to_apply=%bitcast.53.reduce_sub_computation | reduce | bytes 65540
  294.8 3.0 reshape.58
  297.8 10.1 %all_to_all.18 = f32[4,1,2048]{2,1,0:T(1,128)S(1)} all-to-all(f32[4,1,2048]{2,1,0:T(1,128)S(1)} %reshape.58), channel_id=1, replica_groups=mesh['grp'=2,'seq'=4,'pair'=4] {'pair'}, dimensions={0} | all-to-all | bytes 65536 | tf_op jit(solution)/shard_map/all_to_all | solution.py:143
  307.9 0.7 reduce.8
  308.6 4.5 %reshape.59 = f32[4096,1,2]{2,1,0:T(1,128)} reshape(f32[4,2048]{1,0:T(4,128)S(1)} %reduce.8) | data formatting | bytes 65536
  313.1 2.2 copy.28
  315.3 0.7 log-plus-one_subtract_fusion
  (13 shorter events, 0.1 us)
Async XLA Ops:
  6.5 1.5 copy-start
  6.5 1.0 copy-start.1
  6.5 1.5 copy-start.5
  6.5 223.5 %all-gather.4.cloned.1.call-start = ((), (), s32[]{:S(2)}) async-start(), calls=%async_computation.1 | async-start | bytes 15728640 | tf_op jit(solution)/shard_map/all_gather | solution.py:132
  7.3 10.7 %copy-start.2 = (bf16[1536,512]{1,0:T(8,128)(2,1)S(1)}, bf16[1536,512]{1,0:T(8,128)(2,1)}, u32[]{:S(2)}) copy-start(bf16[1536,512]{1,0:T(8,128)(2,1)} %param.16) | copy-start | bytes 4718596
  7.3 262.1 %all-reduce.3.cloned.1.call-start = ((), (), s32[]{:S(2)}) async-start(), calls=%async_computation.2 | async-start | bytes 262144
  22.6 10.1 %copy-start.3 = (bf16[256,512]{0,1:T(8,128)(2,1)S(1)}, bf16[256,512]{0,1:T(8,128)(2,1)}, u32[]{:S(2)}) copy-start(bf16[256,512]{0,1:T(8,128)(2,1)} %copy.23) | copy-start | bytes 786436
  35.3 1.0 copy-start.4
  35.3 4.6 %copy-start.7 = (s32[2,64]{1,0:T(2,128)S(1)}, s32[2,64]{1,0:T(2,128)}, u32[]{:S(2)}) copy-start(s32[2,64]{1,0:T(2,128)} %param.23) | copy-start | bytes 1540
  35.3 4.6 %copy-start.8 = (s32[2,64]{1,0:T(2,128)S(1)}, s32[2,64]{1,0:T(2,128)}, u32[]{:S(2)}) copy-start(s32[2,64]{1,0:T(2,128)} %param.22) | copy-start | bytes 1540
  35.4 4.6 %copy-start.9 = (s32[2,8]{1,0:T(2,128)S(1)}, s32[2,8]{1,0:T(2,128)}, u32[]{:S(2)}) copy-start(s32[2,8]{1,0:T(2,128)} %param.25) | copy-start | bytes 196
  35.6 6.2 %copy-start.6 = (f32[1024]{0:T(1024)S(1)}, f32[1024]{0:T(1024)}, u32[]{:S(2)}) copy-start(f32[1024]{0:T(1024)} %param.21) | copy-start | bytes 12292
  36.4 24.5 %collective-permute-start = (f32[1,1536]{1,0:T(1,128)S(1)}, f32[1,1536]{1,0:T(1,128)S(1)}, u32[]{:S(2)}, u32[]{:S(2)}) collective-permute-start(f32[1,1536]{1,0:T(1,128)S(1)} %get-tuple-element.8), channel_id=1, source_target_pairs={{0,4},{4,8},{8,12},{1,5},{5,9},{9,13},{2,6},{6,10},{10,14},{3,7},{... | collective-permute-start | bytes 18440 | tf_op jit(solution)/shard_map/ppermute | solution.py:21
  38.6 22.3 %collective-permute-start.1 = (f32[1,1536]{1,0:T(1,128)S(1)}, f32[1,1536]{1,0:T(1,128)S(1)}, u32[]{:S(2)}, u32[]{:S(2)}) collective-permute-start(f32[1,1536]{1,0:T(1,128)S(1)} %get-tuple-element.9), channel_id=1, source_target_pairs={{4,0},{8,4},{12,8},{5,1},{9,5},{13,9},{6,2},{10,6},{14,10},{7,3},{... | collective-permute-start | bytes 18440 | tf_op jit(solution)/shard_map/ppermute | solution.py:24
  236.8 2.9 copy-start.10
Sparse Core Ops, SparseCore 0:
  8.9 221.0 all-gather.3
  239.7 29.5 all-reduce.2
where the time goes:
time: 323 us
  waiting for transfers between devices  198 us (61%)
  blocking collectives  45.6 us (14%)
  other arithmetic  22.5 us (7%)
  local copies, waits for them, and re-layouts  21.2 us (7%)
  matrix products  17.2 us (5%)
  between operations  14.4 us (4%)
  starting transfers between devices  3.59 us (1%)
    all_gather x1, waiting for transfers between devices, body(): lax.all_gather(head_weight, 'pair', axis=1, tiled=True)  169 us
    unnamed x3, waiting for transfers between devices  29.2 us
    unnamed x1, other arithmetic  20.4 us
    all_gather x1, blocking collectives, body(): lax.all_gather(head_bias.astype(jnp.bfloat16), 'pair', axis=0, tiled=True)  19.1 us
    all_to_all x1, blocking collectives, body(): lax.all_to_all(gene_cover, 'pair', split_axis=2, concat_axis=0, tiled=True)  10.1 us
    unnamed x27, local copies, waits for them, and re-layouts  10 us
    all_gather x1, blocking collectives, body(): lax.all_gather(values_local[None], 'seq', axis=1, tiled=True)[0]  8.84 us
    all_gather x1, blocking collectives, body(): lax.all_gather(keys_local[None], 'seq', axis=1, tiled=True)[0]  7.67 us
  transfers between devices with their start and end apart: 4, of which 2 were waited for; matrix products, arithmetic and copies ran while one was open for 4% of the time, Pallas kernels for 0%

commit v1 on v0

v1 whole, which is shorter than its diff:
```python
import functools
import math

import jax
import jax.numpy as jnp
from jax import lax
from jax.experimental import pallas as pl
from jax.experimental.pallas import tpu as pltpu
from jax.sharding import PartitionSpec as P

HEADS = 8
KEY = 64
VALUE = 192
EPSILON = 1e-05
HALO = 16
GROUP = 2
CHUNKS = HEADS // GROUP
KCOLS = GROUP * KEY
VCOLS = GROUP * VALUE
TILE = 256
MESH = pl.DeviceIdType.MESH
BF16 = jnp.bfloat16
F32 = jnp.float32


def normalise(rows, gain):
    wide = rows.astype(F32)
    center = jnp.mean(wide, axis=-1, keepdims=True)
    spread_sq = jnp.mean(jnp.square(wide - center), axis=-1, keepdims=True)
    return ((wide - center) * lax.rsqrt(spread_sq + EPSILON) * gain).astype(BF16)


def softplus(x):
    return jnp.maximum(x, 0.0) + jnp.log1p(jnp.exp(-jnp.abs(x)))


def kernel(
    S,
    Z,
    x_ref,
    skip_ref,
    gain_ref,
    conv_ref,
    bias_ref,
    start_ref,
    length_ref,
    gene_ref,
    order_ref,
    wq_hbm,
    wk_hbm,
    wv_hbm,
    wh_hbm,
    out_ref,
    wq,
    wk,
    wv,
    wh,
    xall,
    xq,
    normed,
    normed_q,
    mixed,
    select,
    masks,
    feat,
    cover,
    landed,
    w_sem,
    x_send,
    x_recv,
    halo_send,
    halo_recv,
    up_send,
    down_send,
    f_recv,
    c_send,
    c_recv,
):
    bins, width = x_ref.shape
    out_bins = 2 * bins
    variants, exons = start_ref.shape
    genes = order_ref.shape[1]
    per_owner = genes // S
    owner_rows = Z * per_owner
    half_rows = owner_rows // 2
    tracks = wh.shape[1]
    q_rows = bins + 2 * HALO

    me = lax.axis_index("seq")
    z = lax.axis_index("pair")
    row, core = me // 2, me % 2
    sibling = row * 2 + (1 - core)
    left, right = (me + S - 1) % S, (me + 1) % S
    has_up, has_down = z < Z - 1, z > 0

    loads = [
        pltpu.make_async_copy(src, dst, w_sem.at[i])
        for i, (src, dst) in enumerate(
            ((wq_hbm, wq), (wk_hbm, wk), (wv_hbm, wv), (wh_hbm, wh))
        )
    ]
    for load in loads:
        load.start()

    barrier = pltpu.get_barrier_semaphore()
    for d in range(1, S):
        pl.semaphore_signal(barrier, inc=1, device_id={"seq": (me + d) % S}, device_id_type=MESH)

    @pl.when(has_up)
    def _():
        pl.semaphore_signal(barrier, inc=1, device_id={"pair": z + 1}, device_id_type=MESH)

    @pl.when(has_down)
    def _():
        pl.semaphore_signal(barrier, inc=1, device_id={"pair": z - 1}, device_id_type=MESH)

    line = jnp.where(has_up, 1, 0) + jnp.where(has_down, 1, 0)
    pl.semaphore_wait(barrier, S - 1 + line)

    rows_n = S // 2

    def x_copy(src, slot, sem, target):
        return pltpu.make_async_remote_copy(
            src_ref=src,
            dst_ref=xall.at[slot],
            send_sem=x_send.at[sem],
            recv_sem=x_recv.at[slot],
            device_id={"seq": target},
            device_id_type=MESH,
        )

    sends = []
    for d in range(1, rows_n):
        sends.append(x_copy(x_ref, me, d, ((row + d) % rows_n) * 2 + core))
    sends.append(x_copy(x_ref, me, 0, sibling))
    skip_low = bins + 2 * HALO
    skip_own = skip_low + HALO
    skip_high = skip_own + out_bins
    sends.append(
        pltpu.make_async_remote_copy(
            src_ref=skip_ref.at[pl.ds(0, HALO)],
            dst_ref=mixed.at[pl.ds(skip_high, HALO)],
            send_sem=halo_send.at[0],
            recv_sem=halo_recv.at[0],
            device_id={"seq": left},
            device_id_type=MESH,
        )
    )
    sends.append(
        pltpu.make_async_remote_copy(
            src_ref=skip_ref.at[pl.ds(out_bins - HALO, HALO)],
            dst_ref=mixed.at[pl.ds(skip_low, HALO)],
            send_sem=halo_send.at[1],
            recv_sem=halo_recv.at[1],
            device_id={"seq": right},
            device_id_type=MESH,
        )
    )
    halos = sends[-2:]
    for copy in sends:
        copy.start()

    gain = gain_ref[...]
    xall[me] = x_ref[...]
    mixed[skip_own:skip_high] = skip_ref[...]
    normed[me] = normalise(x_ref[...], gain)
    cover[...] = jnp.zeros_like(cover)

    pick_row = lax.broadcasted_iota(jnp.int32, (3 * out_bins, mixed.shape[0]), 0)
    pick_col = lax.broadcasted_iota(jnp.int32, (3 * out_bins, mixed.shape[0]), 1)
    offset = pick_row % out_bins + pick_row // out_bins - 1
    place = me * out_bins + offset
    chosen = (pick_col == (offset + 2 * HALO) // 2) | (pick_col == offset + skip_own)
    chosen = chosen & (place >= 0) & (place < S * out_bins)
    select[...] = jnp.where(chosen, 1.0, 0.0).astype(BF16)

    eye = lax.broadcasted_iota(jnp.int32, (exons, exons), 0) == lax.broadcasted_iota(
        jnp.int32, (exons, exons), 1
    )
    position = me * out_bins + lax.broadcasted_iota(jnp.int32, (exons, out_bins), 1)
    mask_rows = S * owner_rows
    r = lax.broadcasted_iota(jnp.int32, (mask_rows, genes), 0)
    wanted = (r // owner_rows) * per_owner + r % per_owner
    hot = wanted == lax.broadcasted_iota(jnp.int32, (mask_rows, genes), 1)
    for v in range(variants):
        starts = jnp.broadcast_to(start_ref[v : v + 1, :], (exons, exons))
        lengths = jnp.broadcast_to(length_ref[v : v + 1, :], (exons, exons))
        lower = jnp.sum(jnp.where(eye, starts, 0).astype(F32), axis=1, keepdims=True)
        extent = jnp.sum(jnp.where(eye, lengths, 0).astype(F32), axis=1, keepdims=True)
        where = position.astype(F32)
        inside = jnp.where((where >= lower) & (where < lower + extent), 1.0, 0.0).astype(BF16)
        orders = jnp.broadcast_to(order_ref[v : v + 1, :], (mask_rows, genes))
        gene = jnp.sum(jnp.where(hot, orders, 0).astype(F32), axis=1, keepdims=True)
        owned = jnp.broadcast_to(gene_ref[v : v + 1, :], (mask_rows, exons)).astype(F32)
        match = jnp.where(owned == gene, 1.0, 0.0).astype(BF16)
        masks[v] = jnp.dot(match, inside, preferred_element_type=F32)

    for d in range(1, rows_n):
        slot = ((row + rows_n - d) % rows_n) * 2 + core
        x_copy(x_ref, slot, d, sibling).wait_recv()
        forward = x_copy(xall.at[slot], slot, rows_n + d, sibling)
        forward.start()
        sends.append(forward)
        normed[slot] = normalise(xall[slot], gain)
    for d in range(rows_n):
        slot = ((row + rows_n - d) % rows_n) * 2 + (1 - core)
        x_copy(x_ref, slot, d, sibling).wait_recv()
        normed[slot] = normalise(xall[slot], gain)
    for source, target in ((xall, xq), (normed, normed_q)):
        target[0:HALO] = source[left, bins - HALO : bins]
        target[HALO : HALO + bins] = source[me]
        target[HALO + bins : q_rows] = source[right, 0:HALO]
    for halo in halos:
        halo.wait_recv()
    for load in loads[:3]:
        load.wait()

    def block_copy(block, chunk, sem, target):
        view = feat.at[block, :, pl.ds(pl.multiple_of(chunk * VCOLS, 128), VCOLS)]
        return pltpu.make_async_remote_copy(
            src_ref=view,
            dst_ref=view,
            send_sem=sem.at[block, chunk],
            recv_sem=f_recv.at[block, chunk],
            device_id={"pair": target},
            device_id_type=MESH,
        )

    def send_up(block, chunk):
        @pl.when(has_up)
        def _():
            block_copy(block, chunk, up_send, z + 1).start()

    def send_down(block, chunk):
        @pl.when(has_down)
        def _():
            block_copy(block, chunk, down_send, z - 1).start()

    def arrive(distance, chunk):
        @pl.when(z - distance >= 0)
        def _():
            block_copy(z - distance, chunk, up_send, z - 1).wait_recv()
            send_up(z - distance, chunk)

        @pl.when(z + distance < Z)
        def _():
            block_copy(z + distance, chunk, down_send, z + 1).wait_recv()
            send_down(z + distance, chunk)

    all_rows = S * bins
    inv_root = 1.0 / math.sqrt(KEY)

    def attend(chunk, carry):
        kcols = pl.ds(pl.multiple_of(chunk * KCOLS, 128), KCOLS)
        vcols = pl.ds(pl.multiple_of(chunk * VCOLS, 128), VCOLS)
        everything = normed[...].reshape(all_rows, width)
        q = jnp.dot(normed_q[...], wq[:, kcols], preferred_element_type=F32)
        k = jnp.dot(everything, wk[:, kcols], preferred_element_type=F32).astype(BF16)
        v = jnp.dot(everything, wv[:, vcols], preferred_element_type=F32).astype(BF16)
        lane = lax.broadcasted_iota(jnp.int32, (q_rows, KCOLS), 1)
        stacked = jnp.concatenate(
            [jnp.where(lane // KEY == h, q, 0.0).astype(BF16) for h in range(GROUP)], axis=0
        )
        logits = (
            lax.dot_general(stacked, k, (((1,), (1,)), ((), ())), preferred_element_type=F32)
            * inv_root
        )
        expo = jnp.exp(logits - jnp.max(logits, axis=-1, keepdims=True))
        denom = jnp.sum(expo, axis=-1, keepdims=True)
        mix = jnp.dot(expo.astype(BF16), v, preferred_element_type=F32) / denom
        column = lax.broadcasted_iota(jnp.int32, (q_rows, VCOLS), 1)
        attention = jnp.where(column < VALUE, mix[:q_rows], mix[q_rows:])
        mixed[0:q_rows, vcols] = (xq[:, vcols].astype(F32) + attention).astype(BF16)
        taps = jnp.dot(select[...], mixed[:, vcols], preferred_element_type=F32)
        weight = conv_ref[:, vcols]
        convolved = (
            weight[0:1] * taps[:out_bins]
            + weight[1:2] * taps[out_bins : 2 * out_bins]
            + weight[2:3] * taps[2 * out_bins :]
        )
        feat[z, :, vcols] = jax.nn.gelu(convolved, approximate=True).astype(BF16)
        send_up(z, chunk)
        send_down(z, chunk)

        @pl.when(chunk >= 1)
        def _():
            arrive(1, chunk - 1)

        return carry

    lax.fori_loop(0, CHUNKS, attend, 0)
    arrive(1, CHUNKS - 1)
    loads[3].wait()

    index = lax.broadcasted_iota(jnp.int32, (mask_rows, out_bins), 0) % owner_rows
    sequence = 2 * ((index % half_rows) // per_owner) + index // half_rows

    def score(block):
        mask = jnp.where(sequence == block, masks[block // 2], 0.0).astype(BF16)
        mask = jnp.concatenate([mask, mask], axis=1)

        def tile(n, carry):
            cols = pl.ds(pl.multiple_of(n * TILE, 128), TILE)
            raw = jnp.dot(feat[block], wh[:, cols], preferred_element_type=F32)
            predicted = softplus(raw + bias_ref[:, cols])
            high = predicted.astype(BF16)
            low = (predicted - high.astype(F32)).astype(BF16)
            part = jnp.dot(
                mask, jnp.concatenate([high, low], axis=0), preferred_element_type=F32
            )
            cover[:, :, cols] += part.reshape(S, owner_rows, TILE)
            return carry

        lax.fori_loop(0, tracks // TILE, tile, 0)

    score(z)

    def spread(distance, carry):
        @pl.when(distance + 1 < Z)
        def _():
            for chunk in range(CHUNKS):
                arrive(distance + 1, chunk)

        @pl.when(z - distance >= 0)
        def _():
            score(z - distance)

        @pl.when(z + distance < Z)
        def _():
            score(z + distance)

        return carry

    lax.fori_loop(1, Z, spread, 0)

    def cover_copy(src, slot, sem, target):
        return pltpu.make_async_remote_copy(
            src_ref=cover.at[src],
            dst_ref=landed.at[slot],
            send_sem=c_send.at[sem],
            recv_sem=c_recv.at[slot],
            device_id={"seq": target},
            device_id_type=MESH,
        )

    for d in range(1, S):
        target = (me + d) % S
        copy = cover_copy(target, me, d, target)
        copy.start()
        sends.append(copy)
    total = cover[me]
    for d in range(1, S):
        source = (me + S - d) % S
        cover_copy(source, source, d, source).wait_recv()
        total = total + landed[source]
    logs = jnp.log1p(total)
    scores = logs[half_rows:] - logs[:half_rows]
    for v in range(variants):
        out_ref[v] = scores[v * per_owner : (v + 1) * per_owner]

    for copy in sends:
        copy.wait_send()

    def settle(block, carry):
        for chunk in range(CHUNKS):
            @pl.when(has_up & (block <= z))
            def _():
                block_copy(block, chunk, up_send, z + 1).wait_send()

            @pl.when(has_down & (block >= z))
            def _():
                block_copy(block, chunk, down_send, z - 1).wait_send()

        return carry

    lax.fori_loop(0, Z, settle, 0)


def body(
    S,
    Z,
    seq_input,
    skip_input,
    norm_gain,
    query_weight,
    key_weight,
    value_weight,
    conv_weight,
    head_weight,
    head_bias,
    exon_start,
    exon_length,
    exon_gene,
    gene_order,
):
    bins, width = seq_input.shape[1:]
    tracks = head_weight.shape[1]
    variants = exon_start.shape[0]
    per_owner = gene_order.shape[1] // S
    owner_rows = Z * per_owner
    q_rows = bins + 2 * HALO
    mixed_rows = q_rows + 2 * bins + 2 * HALO
    vmem = pl.BlockSpec(memory_space=pltpu.VMEM)
    hbm = pl.BlockSpec(memory_space=pl.ANY)
    dma = pltpu.SemaphoreType.DMA
    return pl.pallas_call(
        functools.partial(kernel, S, Z),
        out_shape=jax.ShapeDtypeStruct((variants, per_owner, tracks), F32),
        in_specs=[vmem] * 9 + [hbm] * 4,
        out_specs=vmem,
        scratch_shapes=[
            pltpu.VMEM(query_weight.shape, BF16),
            pltpu.VMEM(key_weight.shape, BF16),
            pltpu.VMEM(value_weight.shape, BF16),
            pltpu.VMEM(head_weight.shape, BF16),
            pltpu.VMEM((S, bins, width), BF16),
            pltpu.VMEM((q_rows, width), BF16),
            pltpu.VMEM((S, bins, width), BF16),
            pltpu.VMEM((q_rows, width), BF16),
            pltpu.VMEM((mixed_rows, width), BF16),
            pltpu.VMEM((6 * bins, mixed_rows), BF16),
            pltpu.VMEM((variants, S * owner_rows, 2 * bins), F32),
            pltpu.VMEM((Z, 2 * bins, width), BF16),
            pltpu.VMEM((S, owner_rows, tracks), F32),
            pltpu.VMEM((S, owner_rows, tracks), F32),
            dma((4,)),
            dma((S,)),
            dma((S,)),
            dma((2,)),
            dma((2,)),
            dma((Z, CHUNKS)),
            dma((Z, CHUNKS)),
            dma((Z, CHUNKS)),
            dma((S,)),
            dma((S,)),
        ],
        compiler_params=pltpu.CompilerParams(
            collective_id=0, has_side_effects=True, vmem_limit_bytes=56 * 1024 * 1024
        ),
    )(
        seq_input[0],
        skip_input[0],
        norm_gain[None],
        conv_weight,
        head_bias[None],
        exon_start,
        exon_length,
        exon_gene,
        gene_order,
        query_weight,
        key_weight,
        value_weight,
        head_weight,
    )


def solution(mesh):
    placed = (
        P(("grp", "pair"), "seq", None),
        P(("grp", "pair"), "seq", None),
        P(),
        P(),
        P(),
        P(),
        P(),
        P(None, "pair"),
        P("pair"),
        P("grp", None),
        P("grp", None),
        P("grp", None),
        P("grp", None),
    )
    return jax.shard_map(
        functools.partial(body, mesh.shape["seq"], mesh.shape["pair"]),
        mesh=mesh,
        in_specs=placed,
        out_specs=P("grp", "seq", "pair"),
        check_vma=False,
    )
```

time: 323 us -> 53.5 us (0.17)
  waiting for transfers between devices: 198 us -> 0 us
  Pallas kernels: 0 us -> 50.6 us
  blocking collectives: 45.6 us -> 0 us
  other arithmetic: 22.5 us -> 0 us
  local copies, waits for them, and re-layouts: 21.2 us -> 2.62 us
  matrix products: 17.2 us -> 0 us
  between operations: 14.4 us -> 0.01 us
  starting transfers between devices: 3.59 us -> 0 us
    all_gather x1 -> x0, waiting for transfers between devices: 169 us -> none  [body(): lax.all_gather(head_weight, 'pair', axis=1, tiled=True)]
    pallas_call x0 -> x1, Pallas kernels: none -> 50.6 us  [body(): pl.pallas_call(functools.partial(kernel, S, Z), out_shape=jax.ShapeDtypeS...]
    all_gather x3 -> x0, blocking collectives: 35.6 us -> none  [the longest x1 19.1 us: body(): lax.all_gather(head_bias.astype(jnp.bfloat16), 'pair', axis=0, tiled=True)]
    unnamed x3 -> x0, waiting for transfers between devices: 29.2 us -> none
    unnamed x1 -> x0, other arithmetic: 20.4 us -> none
    dot_general x8 -> x0, matrix products: 17.2 us -> none  [the longest x1 6.73 us: body(): jnp.dot(feature, full_weight, preferred_element_type=jnp.float32)]
    all_to_all x1 -> x0, blocking collectives: 10.1 us -> none  [body(): lax.all_to_all(gene_cover, 'pair', split_axis=2, concat_axis=0, tiled=True)]
    unnamed x27 -> x1, local copies, waits for them, and re-layouts: 10 us -> 1.32 us
  transfers between devices with their start and end apart: 4 -> 0, of which waited for: 2 -> 0; matrix products, arithmetic and copies ran while one was open for 4% -> 0% of each run, Pallas kernels for 0% -> 0%
where the time goes in v1:
time: 53.5 us; the launch traced here: 53.2 us
  Pallas kernels  50.6 us (95%)
  local copies, waits for them, and re-layouts  2.62 us (5%)
    pallas_call x1, Pallas kernels, body(): pl.pallas_call(functools.partial(kernel, S, Z), out_shape=jax.ShapeDtypeS...  50.6 us
    unnamed x1, local copies, waits for them, and re-layouts  1.32 us
    broadcast_in_dim x1, local copies, waits for them, and re-layouts, body(): norm_gain[None]  1.29 us

profile of v1, /device:TPU:0, one launch (start us, length us, event | category | flops | bytes accessed | tf_op | source)
XLA Modules:
  0.0 53.2 jit_solution(14455258780674327441)
XLA Ops:
  0.0 1.3 %broadcast_in_dim.6.gain_ref = f32[1,1536]{1,0:T(1,128)} reshape(f32[1536]{0:T(1024)} %param.15) | data formatting | bytes 12288 | tf_op jit(solution)/shard_map/broadcast_in_dim | solution.py:443
  1.3 50.6 %shard_map.127 = f32[2,2,1024]{2,1,0:T(2,128)} custom-call(bf16[64,1536]{1,0:T(8,128)(2,1)} %bitcast.4, bf16[128,1536]{1,0:T(8,128)(2,1)} %bitcast.3, f32[1,1536]{1,0:T(1,128)} %broadcast_in_dim.6.gain_ref, f32[3,1536]{1,0:T(4,128)} %conv_ref.1, f32[1,1024]{1,0:T(1,128)} %bitcast.5, s32[2,64]{1,0:T(2,128)} %start_ref.1, s32[2,64]{1,0:T(2,128)} %length_ref.1, ...), custom_call_target="tpu_custom_call" | custom-call | tf_op jit(solution)/shard_map/pallas_call | solution.py:406
  51.9 1.3 %copy.15 = f32[2,2,1024]{2,1,0:T(2,128)} copy(f32[2,2,1024]{2,1,0:T(2,128)} %shard_map.127) | data formatting | bytes 32768

commit v2 on v1

--- a/solution.py
+++ b/solution.py
@@ -18,6 +18,7 @@
 KCOLS = GROUP * KEY
 VCOLS = GROUP * VALUE
 TILE = 256
+PARTS = 2
 MESH = pl.DeviceIdType.MESH
 BF16 = jnp.bfloat16
 F32 = jnp.float32
@@ -37,8 +38,8 @@
 def kernel(
     S,
     Z,
-    x_ref,
-    skip_ref,
+    x_hbm,
+    skip_hbm,
     gain_ref,
     conv_ref,
     bias_ref,
@@ -63,6 +64,7 @@
     select,
     masks,
     feat,
+    raw,
     cover,
     landed,
     w_sem,
@@ -76,7 +78,7 @@
     c_send,
     c_recv,
 ):
-    bins, width = x_ref.shape
+    bins, width = x_hbm.shape
     out_bins = 2 * bins
     variants, exons = start_ref.shape
     genes = order_ref.shape[1]
@@ -93,14 +95,23 @@
     left, right = (me + S - 1) % S, (me + 1) % S
     has_up, has_down = z < Z - 1, z > 0
 
+    skip_low = bins + 2 * HALO
+    skip_own = skip_low + HALO
+    skip_high = skip_own + out_bins
     loads = [
         pltpu.make_async_copy(src, dst, w_sem.at[i])
         for i, (src, dst) in enumerate(
-            ((wq_hbm, wq), (wk_hbm, wk), (wv_hbm, wv), (wh_hbm, wh))
+            (
+                (x_hbm, xall.at[me]),
+                (skip_hbm, mixed.at[pl.ds(skip_own, out_bins)]),
+                (wk_hbm, wk),
+                (wv_hbm, wv),
+                (wq_hbm, wq),
+                (wh_hbm, wh),
+            )
         )
     ]
-    for load in loads:
-        load.start()
+    loads[0].start()
 
     barrier = pltpu.get_barrier_semaphore()
     for d in range(1, S):
@@ -119,26 +130,28 @@
 
     rows_n = S // 2
 
-    def x_copy(src, slot, sem, target):
+    part_rows = bins // PARTS
+
+    def x_copy(src, slot, part, sem, target):
+        piece = pl.ds(part * part_rows, part_rows)
         return pltpu.make_async_remote_copy(
-            src_ref=src,
-            dst_ref=xall.at[slot],
-            send_sem=x_send.at[sem],
-            recv_sem=x_recv.at[slot],
+            src_ref=src.at[piece],
+            dst_ref=xall.at[slot, piece],
+            send_sem=x_send.at[sem, part],
+            recv_sem=x_recv.at[slot, part],
             device_id={"seq": target},
             device_id_type=MESH,
         )
 
     sends = []
-    for d in range(1, rows_n):
-        sends.append(x_copy(x_ref, me, d, ((row + d) % rows_n) * 2 + core))
-    sends.append(x_copy(x_ref, me, 0, sibling))
-    skip_low = bins + 2 * HALO
-    skip_own = skip_low + HALO
-    skip_high = skip_own + out_bins
+    for part in range(PARTS):
+        for d in range(1, rows_n):
+            sends.append(x_copy(x_hbm, me, part, d, ((row + d) % rows_n) * 2 + core))
+    for part in range(PARTS):
+        sends.append(x_copy(x_hbm, me, part, 0, sibling))
     sends.append(
         pltpu.make_async_remote_copy(
-            src_ref=skip_ref.at[pl.ds(0, HALO)],
+            src_ref=skip_hbm.at[pl.ds(0, HALO)],
             dst_ref=mixed.at[pl.ds(skip_high, HALO)],
             send_sem=halo_send.at[0],
             recv_sem=halo_recv.at[0],
@@ -148,7 +161,7 @@
     )
     sends.append(
         pltpu.make_async_remote_copy(
-            src_ref=skip_ref.at[pl.ds(out_bins - HALO, HALO)],
+            src_ref=skip_hbm.at[pl.ds(out_bins - HALO, HALO)],
             dst_ref=mixed.at[pl.ds(skip_low, HALO)],
             send_sem=halo_send.at[1],
             recv_sem=halo_recv.at[1],
@@ -159,11 +172,12 @@
     halos = sends[-2:]
     for copy in sends:
         copy.start()
-
-    gain = gain_ref[...]
-    xall[me] = x_ref[...]
-    mixed[skip_own:skip_high] = skip_ref[...]
-    normed[me] = normalise(x_ref[...], gain)
+    for load in loads[1:]:
+        load.start()
+
+    gain = gain_ref[...].reshape(1, width)
+    loads[0].wait()
+    normed[me] = normalise(xall[me], gain)
     cover[...] = jnp.zeros_like(cover)
 
     pick_row = lax.broadcasted_iota(jnp.int32, (3 * out_bins, mixed.shape[0]), 0)
@@ -195,24 +209,28 @@
         match = jnp.where(owned == gene, 1.0, 0.0).astype(BF16)
         masks[v] = jnp.dot(match, inside, preferred_element_type=F32)
 
-    for d in range(1, rows_n):
-        slot = ((row + rows_n - d) % rows_n) * 2 + core
-        x_copy(x_ref, slot, d, sibling).wait_recv()
-        forward = x_copy(xall.at[slot], slot, rows_n + d, sibling)
-        forward.start()
-        sends.append(forward)
-        normed[slot] = normalise(xall[slot], gain)
+    for part in range(PARTS):
+        for d in range(1, rows_n):
+            slot = ((row + rows_n - d) % rows_n) * 2 + core
+            x_copy(x_hbm, slot, part, d, sibling).wait_recv()
+            forward = x_copy(xall.at[slot], slot, part, rows_n + d, sibling)
+            forward.start()
+            sends.append(forward)
+            piece = pl.ds(part * part_rows, part_rows)
+            normed[slot, piece] = normalise(xall[slot, piece], gain)
     for d in range(rows_n):
         slot = ((row + rows_n - d) % rows_n) * 2 + (1 - core)
-        x_copy(x_ref, slot, d, sibling).wait_recv()
-        normed[slot] = normalise(xall[slot], gain)
+        for part in range(PARTS):
+            x_copy(x_hbm, slot, part, d, sibling).wait_recv()
+            piece = pl.ds(part * part_rows, part_rows)
+            normed[slot, piece] = normalise(xall[slot, piece], gain)
     for source, target in ((xall, xq), (normed, normed_q)):
         target[0:HALO] = source[left, bins - HALO : bins]
         target[HALO : HALO + bins] = source[me]
         target[HALO + bins : q_rows] = source[right, 0:HALO]
     for halo in halos:
         halo.wait_recv()
-    for load in loads[:3]:
+    for load in loads[1:5]:
         load.wait()
 
     def block_copy(block, chunk, sem, target):
@@ -236,16 +254,25 @@
         def _():
             block_copy(block, chunk, down_send, z - 1).start()
 
-    def arrive(distance, chunk):
-        @pl.when(z - distance >= 0)
+    def relay(distance, chunk):
+        @pl.when(has_up & (z - distance >= 0))
         def _():
             block_copy(z - distance, chunk, up_send, z - 1).wait_recv()
             send_up(z - distance, chunk)
 
-        @pl.when(z + distance < Z)
+        @pl.when(has_down & (z + distance < Z))
         def _():
             block_copy(z + distance, chunk, down_send, z + 1).wait_recv()
             send_down(z + distance, chunk)
+
+    def arrive(block, chunk):
+        @pl.when((block < z) & jnp.logical_not(has_up))
+        def _():
+            block_copy(block, chunk, up_send, z - 1).wait_recv()
+
+        @pl.when((block > z) & jnp.logical_not(has_down))
+        def _():
+            block_copy(block, chunk, down_send, z + 1).wait_recv()
 
     all_rows = S * bins
     inv_root = 1.0 / math.sqrt(KEY)
@@ -284,25 +311,42 @@
 
         @pl.when(chunk >= 1)
         def _():
-            arrive(1, chunk - 1)
+            relay(1, chunk - 1)
 
         return carry
 
     lax.fori_loop(0, CHUNKS, attend, 0)
-    arrive(1, CHUNKS - 1)
-    loads[3].wait()
+    relay(1, CHUNKS - 1)
+    loads[5].wait()
 
     index = lax.broadcasted_iota(jnp.int32, (mask_rows, out_bins), 0) % owner_rows
     sequence = 2 * ((index % half_rows) // per_owner) + index // half_rows
+
+    early = (CHUNKS - 1) * VCOLS
 
     def score(block):
         mask = jnp.where(sequence == block, masks[block // 2], 0.0).astype(BF16)
         mask = jnp.concatenate([mask, mask], axis=1)
 
-        def tile(n, carry):
+        for chunk in range(CHUNKS - 1):
+            arrive(block, chunk)
+
+        def first(n, carry):
             cols = pl.ds(pl.multiple_of(n * TILE, 128), TILE)
-            raw = jnp.dot(feat[block], wh[:, cols], preferred_element_type=F32)
-            predicted = softplus(raw + bias_ref[:, cols])
+            raw[:, cols] = bias_ref[:, cols] + jnp.dot(
+                feat[block, :, :early], wh[:early, cols], preferred_element_type=F32
+            )
+            return carry
+
+        lax.fori_loop(0, tracks // TILE, first, 0)
+        arrive(block, CHUNKS - 1)
+
+        def second(n, carry):
+            cols = pl.ds(pl.multiple_of(n * TILE, 128), TILE)
+            predicted = softplus(
+                raw[:, cols]
+                + jnp.dot(feat[block, :, early:], wh[early:, cols], preferred_element_type=F32)
+            )
             high = predicted.astype(BF16)
             low = (predicted - high.astype(F32)).astype(BF16)
             part = jnp.dot(
@@ -311,7 +355,7 @@
             cover[:, :, cols] += part.reshape(S, owner_rows, TILE)
             return carry
 
-        lax.fori_loop(0, tracks // TILE, tile, 0)
+        lax.fori_loop(0, tracks // TILE, second, 0)
 
     score(z)
 
@@ -319,7 +363,7 @@
         @pl.when(distance + 1 < Z)
         def _():
             for chunk in range(CHUNKS):
-                arrive(distance + 1, chunk)
+                relay(distance + 1, chunk)
 
         @pl.when(z - distance >= 0)
         def _():
@@ -406,7 +450,7 @@
     return pl.pallas_call(
         functools.partial(kernel, S, Z),
         out_shape=jax.ShapeDtypeStruct((variants, per_owner, tracks), F32),
-        in_specs=[vmem] * 9 + [hbm] * 4,
+        in_specs=[hbm] * 2 + [vmem] * 7 + [hbm] * 4,
         out_specs=vmem,
         scratch_shapes=[
             pltpu.VMEM(query_weight.shape, BF16),
@@ -421,11 +465,12 @@
             pltpu.VMEM((6 * bins, mixed_rows), BF16),
             pltpu.VMEM((variants, S * owner_rows, 2 * bins), F32),
             pltpu.VMEM((Z, 2 * bins, width), BF16),
+            pltpu.VMEM((2 * bins, tracks), F32),
             pltpu.VMEM((S, owner_rows, tracks), F32),
             pltpu.VMEM((S, owner_rows, tracks), F32),
-            dma((4,)),
-            dma((S,)),
-            dma((S,)),
+            dma((6,)),
+            dma((S, PARTS)),
+            dma((S, PARTS)),
             dma((2,)),
             dma((2,)),
             dma((Z, CHUNKS)),
@@ -440,7 +485,7 @@
     )(
         seq_input[0],
         skip_input[0],
-        norm_gain[None],
+        norm_gain,
         conv_weight,
         head_bias[None],
         exon_start,

time: 53.5 us -> 49.7 us (0.929)
  Pallas kernels: 50.6 us -> 48.1 us
  local copies, waits for them, and re-layouts: 2.62 us -> 1.32 us
    pallas_call x1, Pallas kernels: 50.6 us -> 48.1 us  [body(): pl.pallas_call(functools.partial(kernel, S, Z), out_shape=jax.ShapeDtypeS...]
    broadcast_in_dim x1 -> x0, local copies, waits for them, and re-layouts: 1.29 us -> none  [body(): norm_gain[None]]
where the time goes in v2:
time: 49.7 us; the launch traced here: 49.5 us
  Pallas kernels  48.1 us (97%)
  local copies, waits for them, and re-layouts  1.32 us (3%)
    pallas_call x1, Pallas kernels, body(): pl.pallas_call(functools.partial(kernel, S, Z), out_shape=jax.ShapeDtypeS...  48.1 us
    unnamed x1, local copies, waits for them, and re-layouts  1.32 us

profile of v2, /device:TPU:0, one launch (start us, length us, event | category | flops | bytes accessed | tf_op | source)
XLA Modules:
  0.0 49.5 jit_solution(18408967758845614012)
XLA Ops:
  0.0 48.1 %shard_map.127 = f32[2,2,1024]{2,1,0:T(2,128)} custom-call(bf16[64,1536]{1,0:T(8,128)(2,1)} %bitcast.4, bf16[128,1536]{1,0:T(8,128)(2,1)} %bitcast.3, f32[1536]{0:T(1024)} %gain_ref.1, f32[3,1536]{1,0:T(4,128)} %conv_ref.1, f32[1,1024]{1,0:T(1,128)} %bitcast.5, s32[2,64]{1,0:T(2,128)} %start_ref.1, s32[2,64]{1,0:T(2,128)} %length_ref.1, s32[2,64]{1,0:T(2,128)} %gene_ref.1, ...), custom_call_target="tpu_custom_call" | custom-call | tf_op jit(solution)/shard_map/pallas_call | solution.py:450
  48.2 1.3 %copy.15 = f32[2,2,1024]{2,1,0:T(2,128)} copy(f32[2,2,1024]{2,1,0:T(2,128)} %shard_map.127) | data formatting | bytes 32768

commit v3 on v2

--- a/solution.py
+++ b/solution.py
@@ -17,7 +17,7 @@
 CHUNKS = HEADS // GROUP
 KCOLS = GROUP * KEY
 VCOLS = GROUP * VALUE
-TILE = 256
+TILE = 512
 PARTS = 2
 MESH = pl.DeviceIdType.MESH
 BF16 = jnp.bfloat16
@@ -315,7 +315,7 @@
 
         return carry
 
-    lax.fori_loop(0, CHUNKS, attend, 0)
+    lax.fori_loop(0, CHUNKS, attend, 0, unroll=True)
     relay(1, CHUNKS - 1)
     loads[5].wait()
 

time: 49.7 us -> 48.7 us (0.980)
  Pallas kernels: 48.1 us -> 47.1 us
    pallas_call x1, Pallas kernels: 48.1 us -> 47.1 us  [body(): pl.pallas_call(functools.partial(kernel, S, Z), out_shape=jax.ShapeDtypeS...]
where the time goes in v3:
time: 48.7 us; the launch traced here: 48.5 us
  Pallas kernels  47.1 us (97%)
  local copies, waits for them, and re-layouts  1.32 us (3%)
    pallas_call x1, Pallas kernels, body(): pl.pallas_call(functools.partial(kernel, S, Z), out_shape=jax.ShapeDtypeS...  47.1 us
    unnamed x1, local copies, waits for them, and re-layouts  1.32 us

profile of v3, /device:TPU:0, one launch (start us, length us, event | category | flops | bytes accessed | tf_op | source)
XLA Modules:
  0.0 48.5 jit_solution(15528245285195045239)
XLA Ops:
  0.0 47.1 %shard_map.127 = f32[2,2,1024]{2,1,0:T(2,128)} custom-call(bf16[64,1536]{1,0:T(8,128)(2,1)} %bitcast.4, bf16[128,1536]{1,0:T(8,128)(2,1)} %bitcast.3, f32[1536]{0:T(1024)} %gain_ref.1, f32[3,1536]{1,0:T(4,128)} %conv_ref.1, f32[1,1024]{1,0:T(1,128)} %bitcast.5, s32[2,64]{1,0:T(2,128)} %start_ref.1, s32[2,64]{1,0:T(2,128)} %length_ref.1, s32[2,64]{1,0:T(2,128)} %gene_ref.1, ...), custom_call_target="tpu_custom_call" | custom-call | tf_op jit(solution)/shard_map/pallas_call | solution.py:450
  47.2 1.3 %copy.15 = f32[2,2,1024]{2,1,0:T(2,128)} copy(f32[2,2,1024]{2,1,0:T(2,128)} %shard_map.127) | data formatting | bytes 32768
